TPU v7x, 256 devices: a whole 4x4x8 slice. The times are simulated.
256 devices in a mesh: shot: 8 (over y, core), gx: 4 (over z_hi), gy: 8 (over z_lo, x).
Axes of the slice: x: 4, y: 4, z: 8 (z_hi: 4, z_lo: 2; z = z_hi * 2 + z_lo), core: 2. Of those that a mesh axis runs over, the one named last changes fastest.
Arguments:
- latent: float32 [32, 24, 4096], P('shot', 'gx', 'gy'), may hold values from -6 to 6
- w_first: float32 [64, 64], replicated, may hold values from -0.75 to 0.75
- w_second: float32 [64, 128], replicated, may hold values from -0.75 to 0.75
- fwd_press: float32 [8, 96, 256, 128], P('shot', 'gx', 'gy'), may hold values from -1.5 to 8
- fwd_vel: float32 [8, 3, 96, 256, 128], P('shot', None, 'gx', 'gy'), may hold values from -1.5 to 8
- adj_press: float32 [8, 96, 256, 128], P('shot', 'gx', 'gy'), may hold values from -1.5 to 8
- adj_vel: float32 [8, 3, 96, 256, 128], P('shot', None, 'gx', 'gy'), may hold values from -1.5 to 8
- src_pos: int32 [3, 8], P(None, 'shot'), may hold values from 0 to 255, as said below
- src_amp: float32 [3, 8], P(None, 'shot'), may hold values from -24 to 24
- rec_pos: int32 [8, 3, 2048], P('shot'), may hold values from 0 to 255, as said below
- observed: float32 [8, 3, 2048], P('shot'), may hold values from -6 to 6
Outputs:
- grad_latent: float32 [32, 24, 4096], P('shot', 'gx', 'gy')
- grad_first: float32 [64, 64], replicated
- grad_second: float32 [64, 128], replicated
Inputs may be any that keep to these rules, and one draw needn't show every extreme that they name: `src_pos`: row 0 is an x cell below 96, row 1 a y cell below 256, row 2 a depth cell below 128. `rec_pos`: component 0 is an x cell below 96, component 1 a y cell below 256, component 2 a depth cell below 128; cells may repeat.
All inputs are finite; a program needn't handle non-finite values.
Results may differ from a plain program's by a relative error of at most 0.0003.
Values sent between devices are 32-bit elements; how exact they have to be, the bound alone decides.
No kernel may reach another device: no remote copies, remote signals or barrier semaphores. Data moves between devices by JAX's collectives and lax.ppermute only.
A program may use at most 64 MiB of HBM per device.

v0:
```python
import jax
import jax.numpy as jnp
from jax import lax
from jax.sharding import PartitionSpec as P

CH = 64
STEPS = 3
coeffs = (1225.0 / 1024.0, -245.0 / 3072.0, 49.0 / 5120.0, -5.0 / 7168.0)


def with_halo(block, sides, width):
    for axis, dim in sides:
        count = lax.axis_size(axis)
        forward = [(i, i + 1) for i in range(count - 1)]
        backward = [(target, source) for source, target in forward]
        low = lax.ppermute(
            lax.slice_in_dim(block, block.shape[dim] - width, None, axis=dim), axis, forward
        )
        high = lax.ppermute(lax.slice_in_dim(block, 0, width, axis=dim), axis, backward)
        block = jnp.concatenate([low, block, high], axis=dim)
    return block


def take_slab(values_in, axis_id, start_at, length):
    return lax.slice_in_dim(values_in, start_at, start_at + length, axis=axis_id)


def diff_plus(extended, axis_id, start_at, length):
    summed = 0.0
    for order, weight in enumerate(coeffs):
        offset = order + 1
        summed = summed + weight * (
            take_slab(extended, axis_id, start_at + offset, length)
            - take_slab(extended, axis_id, start_at - offset + 1, length)
        )
    return summed


def diff_minus(extended, axis_id, start_at, length):
    summed = 0.0
    for order, weight in enumerate(coeffs):
        offset = order + 1
        summed = summed + weight * (
            take_slab(extended, axis_id, start_at + offset - 1, length)
            - take_slab(extended, axis_id, start_at - offset, length)
        )
    return summed


def depth_pad(field_in):
    return jnp.pad(field_in, ((0, 0), (0, 0), (4, 4)))


def rim_x(field_in):
    return with_halo(field_in, (("gx", 0),), 4)


def rim_y(field_in):
    return with_halo(field_in, (("gy", 1),), 4)


def narrow_step(fields, modulus, buoyancy):
    pressure, vel_x, vel_y, vel_z = fields
    size_x, size_y, size_z = pressure.shape
    extended = with_halo(pressure, (("gx", 0), ("gy", 1)), 4)
    grad_x = diff_plus(extended[:, 4 : 4 + size_y], 0, 4, size_x)
    grad_y = diff_plus(extended[4 : 4 + size_x], 1, 4, size_y)
    grad_z = diff_plus(depth_pad(pressure), 2, 4, size_z)
    vel_x = vel_x - buoyancy * grad_x
    vel_y = vel_y - buoyancy * grad_y
    vel_z = vel_z - buoyancy * grad_z
    diverge = (
        diff_minus(rim_x(vel_x), 0, 4, size_x)
        + diff_minus(rim_y(vel_y), 1, 4, size_y)
        + diff_minus(depth_pad(vel_z), 2, 4, size_z)
    )
    pressure = pressure - modulus * diverge
    return (
        (pressure, vel_x, vel_y, vel_z),
        diverge,
        (grad_x, grad_y, grad_z),
        (vel_x, vel_y, vel_z),
    )


def decode(latent, w_first, w_second):
    depth_c, rows_x, merged = latent.shape
    rows_y = merged // CH
    flattened = latent.reshape(-1, CH)
    hidden = jnp.tanh(jnp.dot(flattened, w_first, precision=lax.Precision.HIGHEST))
    outputs = jnp.dot(hidden, w_second, precision=lax.Precision.HIGHEST)
    fine_out = (
        outputs.reshape(depth_c, rows_x, rows_y, 2, 4, 4, 4)
        .transpose(3, 1, 4, 2, 5, 0, 6)
        .reshape(2, rows_x * 4, rows_y * 4, depth_c * 4)
    )
    return (flattened, hidden, fine_out)


def materials(fine_out):
    wave_speed = 0.15 + 0.25 * jax.nn.sigmoid(fine_out[0])
    density = 1.0 + 1.5 * jax.nn.sigmoid(fine_out[1])
    return (density * wave_speed * wave_speed, 1.0 / density)


def decoder_grads(flattened, hidden, fine_out, grad_mod, grad_buoy, w_first, w_second):
    sig_speed = jax.nn.sigmoid(fine_out[0])
    sig_dens = jax.nn.sigmoid(fine_out[1])
    wave_speed = 0.15 + 0.25 * sig_speed
    density = 1.0 + 1.5 * sig_dens
    grad_speed = grad_mod * 2.0 * density * wave_speed
    grad_dens = grad_mod * wave_speed * wave_speed - grad_buoy / (density * density)
    grad_fine = jnp.stack(
        [
            grad_speed * 0.25 * sig_speed * (1.0 - sig_speed),
            grad_dens * 1.5 * sig_dens * (1.0 - sig_dens),
        ]
    )
    size_x, size_y, size_z = (grad_fine.shape[1], grad_fine.shape[2], grad_fine.shape[3])
    grad_out = (
        grad_fine.reshape(2, size_x // 4, 4, size_y // 4, 4, size_z // 4, 4)
        .transpose(5, 1, 3, 0, 2, 4, 6)
        .reshape(-1, 128)
    )
    grad_hidden = jnp.dot(grad_out, w_second.T, precision=lax.Precision.HIGHEST)
    grad_pre = grad_hidden * (1.0 - hidden * hidden)
    grad_latent = jnp.dot(grad_pre, w_first.T, precision=lax.Precision.HIGHEST).reshape(
        size_z // 4, size_x // 4, size_y // 4 * CH
    )
    grad_second = jnp.dot(hidden.T, grad_out, precision=lax.Precision.HIGHEST)
    grad_first = jnp.dot(flattened.T, grad_pre, precision=lax.Precision.HIGHEST)
    return (grad_latent, grad_first, grad_second)


def locate(positions, anchor_x, anchor_y, size_x, size_y):
    local_x = positions[0] - anchor_x
    local_y = positions[1] - anchor_y
    inside = (local_x >= 0) & (local_x < size_x) & (local_y >= 0) & (local_y < size_y)
    return (
        jnp.clip(local_x, 0, size_x - 1),
        jnp.clip(local_y, 0, size_y - 1),
        positions[2],
        inside,
    )


def body(
    latent,
    w_first,
    w_second,
    fwd_press,
    fwd_vel,
    adj_press,
    adj_vel,
    src_pos,
    src_amp,
    rec_pos,
    observed,
):
    size_x, size_y = (fwd_press.shape[1], fwd_press.shape[2])
    anchor_x = lax.axis_index("gx") * size_x
    anchor_y = lax.axis_index("gy") * size_y
    flattened, hidden, fine_out = decode(latent, w_first, w_second)
    slab_mod, slab_buoy = materials(fine_out)
    stacked = lax.all_gather(jnp.stack([slab_mod, slab_buoy]), "shot", axis=3, tiled=True)
    modulus, buoyancy = (stacked[0], stacked[1])

    def prepare(vel_x, vel_y):
        return (vel_x, vel_y)

    def advance(fields):
        return narrow_step(fields, modulus, buoyancy)

    def one_shot(totals, inputs):
        grad_mod, grad_buoy = totals
        (
            start_press,
            start_vel,
            back_press,
            back_vel,
            source,
            amplitudes,
            receivers,
            observed_now,
        ) = inputs
        src_x, src_y, src_z, src_in = locate(source, anchor_x, anchor_y, size_x, size_y)
        rec_x, rec_y, rec_z, rec_in = locate(receivers, anchor_x, anchor_y, size_x, size_y)
        fields = (start_press,) + prepare(start_vel[0], start_vel[1]) + (start_vel[2],)
        stored = []
        misfits = []
        for moment in range(STEPS):
            fields, diverge, slopes, own_vel = advance(fields)
            pressure = (
                fields[0].at[src_x, src_y, src_z].add(jnp.where(src_in, amplitudes[moment], 0.0))
            )
            fields = (pressure,) + fields[1:]
            misfits.append(
                jnp.where(rec_in, pressure[rec_x, rec_y, rec_z] - observed_now[moment], 0.0)
            )
            stored.append((diverge, slopes))
        fields = (back_press,) + prepare(back_vel[0], back_vel[1]) + (back_vel[2],)
        for moment in reversed(range(STEPS)):
            pressure = fields[0].at[rec_x, rec_y, rec_z].add(misfits[moment])
            fields, diverge, slopes, own_vel = advance((pressure,) + fields[1:])
            grad_mod = grad_mod - fields[0] * stored[moment][0]
            grad_buoy = grad_buoy - (
                own_vel[0] * stored[moment][1][0]
                + own_vel[1] * stored[moment][1][1]
                + own_vel[2] * stored[moment][1][2]
            )
        return ((grad_mod, grad_buoy), None)

    zeros = jnp.zeros(modulus.shape, jnp.float32)
    totals, _ignored = lax.scan(
        one_shot,
        (zeros, zeros),
        (fwd_press, fwd_vel, adj_press, adj_vel, src_pos.T, src_amp.T, rec_pos, observed),
    )
    shares = lax.psum_scatter(
        jnp.stack([totals[0], totals[1]]), "shot", scatter_dimension=3, tiled=True
    )
    grad_latent, grad_first, grad_second = decoder_grads(
        flattened, hidden, fine_out, shares[0], shares[1], w_first, w_second
    )
    grad_first, grad_second = lax.psum((grad_first, grad_second), ("shot", "gx", "gy"))
    return (grad_latent, grad_first, grad_second)


def solution(mesh):
    in_specs = (
        P("shot", "gx", "gy"),
        P(),
        P(),
        P("shot", "gx", "gy", None),
        P("shot", None, "gx", "gy", None),
        P("shot", "gx", "gy", None),
        P("shot", None, "gx", "gy", None),
        P(None, "shot"),
        P(None, "shot"),
        P("shot", None, None),
        P("shot", None, None),
    )
    out_specs = (P("shot", "gx", "gy"), P(), P())
    return jax.shard_map(body, mesh=mesh, in_specs=in_specs, out_specs=out_specs, check_vma=False)
```

profile of v0, /device:TPU:1, one launch (start us, length us, event | category | flops | bytes accessed | tf_op | source)
XLA Modules:
  0.0 564.5 jit_solution(9128224476889360385)
XLA Ops:
  8.8 6.3 %collective-permute-start.1 = (f32[4,32,128]{2,1,0:T(8,128)}, f32[4,32,128]{2,1,0:T(8,128)}, u32[]{:S(2)}, u32[]{:S(2)}) collective-permute-start(f32[4,32,128]{2,1,0:T(8,128)} %get-tuple-element.217), channel_id=1, source_target_pairs={{0,8},{8,16},{16,24},{1,9},{9,17},{17,25},{2,10},{10,18},{18,26},{... | collective-permute-start | bytes 196616 | tf_op jit(solution)/shard_map/while/body/eval_jaxpr/ppermute | solution.py:16
  35.5 20.7 %all_gather.3 = f32[2,24,32,128]{2,1,0,3:T(8,128)S(1)} all-gather(f32[2,24,32,16]{2,1,0,3:T(8,128)S(1)} %copy.37), channel_id=1, replica_groups=mesh['shot'=8,'gx'=4,'gy'=8] {'shot'}, dimensions={3}, use_global_device_ids=true | all-gather | bytes 884736 | tf_op jit(solution)/shard_map/all_gather | solution.py:165
  69.6 6.8 %collective-permute-start.2 = (f32[4,32,128]{2,1,0:T(8,128)S(1)}, f32[4,32,128]{2,1,0:T(8,128)S(1)}, u32[]{:S(2)}, u32[]{:S(2)}) collective-permute-start(f32[4,32,128]{2,1,0:T(8,128)S(1)} %get-tuple-element.214), channel_id=1, source_target_pairs={{0,8},{8,16},{16,24},{1,9},{9,17},{17,25},{2,10},{10,18},{18,26},{... | collective-permute-start | bytes 196616 | tf_op jit(solution)/shard_map/while/body/eval_jaxpr/ppermute | solution.py:16
  93.1 5.5 collective-permute-start.9
  120.4 6.6 %collective-permute-start.10 = (f32[4,32,128]{2,1,0:T(8,128)S(1)}, f32[4,32,128]{2,1,0:T(8,128)S(1)}, u32[]{:S(2)}, u32[]{:S(2)}) collective-permute-start(f32[4,32,128]{2,1,0:T(8,128)S(1)} %get-tuple-element.208), channel_id=1, source_target_pairs={{0,8},{8,16},{16,24},{1,9},{9,17},{17,25},{2,10},{10,18},{18,26},{... | collective-permute-start | bytes 196616 | tf_op jit(solution)/shard_map/while/body/eval_jaxpr/ppermute | solution.py:16
  132.9 5.5 collective-permute-start.17
  146.4 6.1 %collective-permute-start.21 = (f32[32,4,128]{2,1,0:T(4,128)S(1)}, f32[32,4,128]{2,1,0:T(4,128)S(1)}, u32[]{:S(2)}, u32[]{:S(2)}) collective-permute-start(f32[32,4,128]{2,1,0:T(4,128)S(1)} %get-tuple-element.172), channel_id=1, source_target_pairs={{0,1},{1,2},{2,3},{3,4},{4,5},{5,6},{6,7},{8,9},{9,10},{10,11},{11... | collective-permute-start | bytes 196616 | tf_op jit(solution)/shard_map/while/body/eval_jaxpr/ppermute | solution.py:16
  153.2 25.6 %gather_fusion.2 = f32[2048]{0:T(1024)} fusion(f32[24,32,128]{2,1,0:T(8,128)S(1)} %scatter-add.39, s32[2048]{0:T(1024)S(1)} %bitcast.153), kind=kCustom, calls=%fused_computation.2 | custom fusion | bytes 40960 | tf_op jit(solution)/shard_map/while/body/eval_jaxpr/gather | solution.py:198
  183.5 7.1 %collective-permute-start.22 = (f32[24,4,128]{2,1,0:T(4,128)S(1)}, f32[24,4,128]{2,1,0:T(4,128)}, u32[]{:S(2)}, u32[]{:S(2)}) collective-permute-start(f32[24,4,128]{2,1,0:T(4,128)S(1)} %get-tuple-element.204), channel_id=1, source_target_pairs={{0,1},{1,2},{2,3},{3,4},{4,5},{5,6},{6,7},{8,9},{9,10},{10,11},{11... | collective-permute-start | bytes 147464 | tf_op jit(solution)/shard_map/while/body/eval_jaxpr/ppermute | solution.py:16
  192.0 6.1 %collective-permute-start.18 = (f32[4,32,128]{2,1,0:T(8,128)S(1)}, f32[4,32,128]{2,1,0:T(8,128)S(1)}, u32[]{:S(2)}, u32[]{:S(2)}) collective-permute-start(f32[4,32,128]{2,1,0:T(8,128)S(1)} %get-tuple-element.202), channel_id=1, source_target_pairs={{0,8},{8,16},{16,24},{1,9},{9,17},{17,25},{2,10},{10,18},{18,26},{... | collective-permute-start | bytes 196616 | tf_op jit(solution)/shard_map/while/body/eval_jaxpr/ppermute | solution.py:16
  199.6 16.9 %gather_fusion.1 = f32[2048]{0:T(1024)S(1)} fusion(f32[24,32,128]{2,1,0:T(8,128)S(1)} %scatter-add.40, s32[2048]{0:T(1024)S(1)} %bitcast.154), kind=kCustom, calls=%fused_computation.1 | custom fusion | bytes 40960 | tf_op jit(solution)/shard_map/while/body/eval_jaxpr/gather | solution.py:198
  221.7 16.9 %gather_fusion = f32[2048]{0:T(1024)S(1)} fusion(f32[24,32,128]{2,1,0:T(8,128)S(1)} %scatter-add.41, s32[2048]{0:T(1024)S(1)} %bitcast.155), kind=kCustom, calls=%fused_computation | custom fusion | bytes 40960 | tf_op jit(solution)/shard_map/while/body/eval_jaxpr/gather | solution.py:198
  239.3 12.0 %scatter_fusion = f32[98304]{0:T(1024)S(1)} fusion(f32[98304]{0:T(1024)S(1)} %bitcast.161, s32[2048]{0:T(1024)S(1)} %broadcast_select_fusion, f32[2048]{0:T(1024)S(1)} %get-tuple-element.227), kind=kCustom, calls=%fused_computation.3 | custom fusion | flops 2048 | bytes 32768
  263.8 5.5 collective-permute-start.29
  288.0 12.0 %scatter_fusion.1 = f32[98304]{0:T(1024)S(1)} fusion(f32[98304]{0:T(1024)S(1)} %copy.62, s32[2048]{0:T(1024)S(1)} %broadcast_select_fusion, f32[2048]{0:T(1024)S(1)} %copy-done.34), kind=kCustom, calls=%fused_computation.4 | custom fusion | flops 2048 | bytes 32768
  309.0 6.5 %collective-permute-start.37 = (f32[32,4,128]{2,1,0:T(4,128)S(1)}, f32[32,4,128]{2,1,0:T(4,128)S(1)}, u32[]{:S(2)}, u32[]{:S(2)}) collective-permute-start(f32[32,4,128]{2,1,0:T(4,128)S(1)} %get-tuple-element.164), channel_id=1, source_target_pairs={{0,1},{1,2},{2,3},{3,4},{4,5},{5,6},{6,7},{8,9},{9,10},{10,11},{11... | collective-permute-start | bytes 196616 | tf_op jit(solution)/shard_map/while/body/eval_jaxpr/ppermute | solution.py:16
  317.5 5.8 %collective-permute-start.38 = (f32[24,4,128]{2,1,0:T(4,128)S(1)}, f32[24,4,128]{2,1,0:T(4,128)S(1)}, u32[]{:S(2)}, u32[]{:S(2)}) collective-permute-start(f32[24,4,128]{2,1,0:T(4,128)S(1)} %get-tuple-element.189), channel_id=1, source_target_pairs={{0,1},{1,2},{2,3},{3,4},{4,5},{5,6},{6,7},{8,9},{9,10},{10,11},{11... | collective-permute-start | bytes 147464 | tf_op jit(solution)/shard_map/while/body/eval_jaxpr/ppermute | solution.py:16
  337.4 12.0 %scatter_fusion.2 = f32[98304]{0:T(1024)S(1)} fusion(f32[98304]{0:T(1024)S(1)} %copy.63, s32[2048]{0:T(1024)S(1)} %broadcast_select_fusion, f32[2048]{0:T(1024)S(1)} %copy-done.33), kind=kCustom, calls=%fused_computation.5 | custom fusion | flops 2048 | bytes 32768
  362.0 6.7 %collective-permute-start.45 = (f32[32,4,128]{2,1,0:T(4,128)S(1)}, f32[32,4,128]{2,1,0:T(4,128)S(1)}, u32[]{:S(2)}, u32[]{:S(2)}) collective-permute-start(f32[32,4,128]{2,1,0:T(4,128)S(1)} %get-tuple-element.160), channel_id=1, source_target_pairs={{0,1},{1,2},{2,3},{3,4},{4,5},{5,6},{6,7},{8,9},{9,10},{10,11},{11... | collective-permute-start | bytes 196616 | tf_op jit(solution)/shard_map/while/body/eval_jaxpr/ppermute | solution.py:16
  377.4 5.7 %collective-permute-start.46 = (f32[24,4,128]{2,1,0:T(4,128)S(1)}, f32[24,4,128]{2,1,0:T(4,128)S(1)}, u32[]{:S(2)}, u32[]{:S(2)}) collective-permute-start(f32[24,4,128]{2,1,0:T(4,128)S(1)} %get-tuple-element.183), channel_id=1, source_target_pairs={{0,1},{1,2},{2,3},{3,4},{4,5},{5,6},{6,7},{8,9},{9,10},{10,11},{11... | collective-permute-start | bytes 147464 | tf_op jit(solution)/shard_map/while/body/eval_jaxpr/ppermute | solution.py:16
  384.6 5.7 %collective-permute-done.47 = f32[24,4,128]{2,1,0:T(4,128)S(1)} collective-permute-done((f32[24,4,128]{2,1,0:T(4,128)S(1)}, f32[24,4,128]{2,1,0:T(4,128)S(1)}, u32[]{:S(2)}, u32[]{:S(2)}) %collective-permute-start.47) | collective-permute-done | bytes 49184 | tf_op jit(solution)/shard_map/while/body/eval_jaxpr/ppermute | solution.py:19
  393.6 64.4 %reduce-scatter.2.cloned.1.call-done = f32[2,24,32,16]{2,1,0,3:T(8,128)} async-done(((f32[2,24,32,128]{2,1,0,3:T(8,128)}), f32[2,24,32,16]{2,1,0,3:T(8,128)}) %reduce-scatter.2.cloned.1.call-update) | async-done | bytes 98320 | tf_op jit(solution)/shard_map/reduce_scatter | solution.py:219
  464.8 8.5 %copy.43 = f32[4,6,8,2,4,4,4]{2,1,0,6,5,4,3:T(8,128)} copy(f32[4,6,8,2,4,4,4]{5,2,6,0,4,1,3:T(8,128)S(1)} %maximum_bitcast_fusion) | data formatting | bytes 196608 | tf_op jit(solution)/shard_map/transpose | solution.py:122
  477.0 79.0 %all-reduce.12 = (f32[64,64]{0,1:T(8,128)S(1)}, f32[64,128]{1,0:T(8,128)}) all-reduce(f32[64,64]{0,1:T(8,128)S(1)} %convolution_bitcast_fusion, f32[64,128]{1,0:T(8,128)S(1)} %fusion.561), channel_id=1, replica_groups=mesh['shot'=8,'gx'=4,'gy'=8] {'shot','gx','gy'}, use_global_device_ids=true, to_apply=%region_5.6 | all-reduce | flops 12288 | bytes 98304 | tf_op jit(solution)/shard_map/psum | solution.py:225
  (272 shorter events, 184.2 us)
Async XLA Ops:
  7.2 450.8 %reduce-scatter.2.cloned.1.call-start = ((), (), s32[]{:S(2)}) async-start(), calls=%async_computation.1 | async-start | bytes 3538944 | tf_op jit(solution)/shard_map/reduce_scatter | solution.py:219
  8.8 50.7 %collective-permute-start.1 = (f32[4,32,128]{2,1,0:T(8,128)}, f32[4,32,128]{2,1,0:T(8,128)}, u32[]{:S(2)}, u32[]{:S(2)}) collective-permute-start(f32[4,32,128]{2,1,0:T(8,128)} %get-tuple-element.217), channel_id=1, source_target_pairs={{0,8},{8,16},{16,24},{1,9},{9,17},{17,25},{2,10},{10,18},{18,26},{... | collective-permute-start | bytes 196616 | tf_op jit(solution)/shard_map/while/body/eval_jaxpr/ppermute | solution.py:16
  15.1 44.3 %collective-permute-start = (f32[4,32,128]{2,1,0:T(8,128)}, f32[4,32,128]{2,1,0:T(8,128)}, u32[]{:S(2)}, u32[]{:S(2)}) collective-permute-start(f32[4,32,128]{2,1,0:T(8,128)} %get-tuple-element.218), channel_id=1, source_target_pairs={{8,0},{16,8},{24,16},{9,1},{17,9},{25,17},{10,2},{18,10},{26,18},{... | collective-permute-start | bytes 196616 | tf_op jit(solution)/shard_map/while/body/eval_jaxpr/ppermute | solution.py:19
  60.2 16.2 %collective-permute-start.4 = (f32[32,4,128]{2,1,0:T(4,128)S(1)}, f32[32,4,128]{2,1,0:T(4,128)S(1)}, u32[]{:S(2)}, u32[]{:S(2)}) collective-permute-start(f32[32,4,128]{2,1,0:T(4,128)S(1)} %get-tuple-element.179), channel_id=1, source_target_pairs={{1,0},{2,1},{3,2},{4,3},{5,4},{6,5},{7,6},{9,8},{10,9},{11,10},{12... | collective-permute-start | bytes 196616 | tf_op jit(solution)/shard_map/while/body/eval_jaxpr/ppermute | solution.py:19
  61.5 14.9 %collective-permute-start.5 = (f32[32,4,128]{2,1,0:T(4,128)S(1)}, f32[32,4,128]{2,1,0:T(4,128)S(1)}, u32[]{:S(2)}, u32[]{:S(2)}) collective-permute-start(f32[32,4,128]{2,1,0:T(4,128)S(1)} %get-tuple-element.180), channel_id=1, source_target_pairs={{0,1},{1,2},{2,3},{3,4},{4,5},{5,6},{6,7},{8,9},{9,10},{10,11},{11... | collective-permute-start | bytes 196616 | tf_op jit(solution)/shard_map/while/body/eval_jaxpr/ppermute | solution.py:16
  68.3 20.4 %collective-permute-start.3 = (f32[4,32,128]{2,1,0:T(8,128)S(1)}, f32[4,32,128]{2,1,0:T(8,128)S(1)}, u32[]{:S(2)}, u32[]{:S(2)}) collective-permute-start(f32[4,32,128]{2,1,0:T(8,128)S(1)} %get-tuple-element.213), channel_id=1, source_target_pairs={{8,0},{16,8},{24,16},{9,1},{17,9},{25,17},{10,2},{18,10},{26,18},{... | collective-permute-start | bytes 196616 | tf_op jit(solution)/shard_map/while/body/eval_jaxpr/ppermute | solution.py:19
  69.6 19.1 %collective-permute-start.2 = (f32[4,32,128]{2,1,0:T(8,128)S(1)}, f32[4,32,128]{2,1,0:T(8,128)S(1)}, u32[]{:S(2)}, u32[]{:S(2)}) collective-permute-start(f32[4,32,128]{2,1,0:T(8,128)S(1)} %get-tuple-element.214), channel_id=1, source_target_pairs={{0,8},{8,16},{16,24},{1,9},{9,17},{17,25},{2,10},{10,18},{18,26},{... | collective-permute-start | bytes 196616 | tf_op jit(solution)/shard_map/while/body/eval_jaxpr/ppermute | solution.py:16
  79.6 9.1 %collective-permute-start.7 = (f32[24,4,128]{2,1,0:T(4,128)S(1)}, f32[24,4,128]{2,1,0:T(4,128)S(1)}, u32[]{:S(2)}, u32[]{:S(2)}) collective-permute-start(f32[24,4,128]{2,1,0:T(4,128)S(1)} %get-tuple-element.215), channel_id=1, source_target_pairs={{1,0},{2,1},{3,2},{4,3},{5,4},{6,5},{7,6},{9,8},{10,9},{11,10},{12... | collective-permute-start | bytes 147464 | tf_op jit(solution)/shard_map/while/body/eval_jaxpr/ppermute | solution.py:19
  112.7 15.8 %collective-permute-start.15 = (f32[24,4,128]{2,1,0:T(4,128)S(1)}, f32[24,4,128]{2,1,0:T(4,128)S(1)}, u32[]{:S(2)}, u32[]{:S(2)}) collective-permute-start(f32[24,4,128]{2,1,0:T(4,128)S(1)} %get-tuple-element.209), channel_id=1, source_target_pairs={{1,0},{2,1},{3,2},{4,3},{5,4},{6,5},{7,6},{9,8},{10,9},{11,10},{12... | collective-permute-start | bytes 147464 | tf_op jit(solution)/shard_map/while/body/eval_jaxpr/ppermute | solution.py:19
  114.0 14.5 %collective-permute-start.14 = (f32[24,4,128]{2,1,0:T(4,128)S(1)}, f32[24,4,128]{2,1,0:T(4,128)S(1)}, u32[]{:S(2)}, u32[]{:S(2)}) collective-permute-start(f32[24,4,128]{2,1,0:T(4,128)S(1)} %get-tuple-element.210), channel_id=1, source_target_pairs={{0,1},{1,2},{2,3},{3,4},{4,5},{5,6},{6,7},{8,9},{9,10},{10,11},{11... | collective-permute-start | bytes 147464 | tf_op jit(solution)/shard_map/while/body/eval_jaxpr/ppermute | solution.py:16
  119.1 9.4 %collective-permute-start.11 = (f32[4,32,128]{2,1,0:T(8,128)S(1)}, f32[4,32,128]{2,1,0:T(8,128)S(1)}, u32[]{:S(2)}, u32[]{:S(2)}) collective-permute-start(f32[4,32,128]{2,1,0:T(8,128)S(1)} %get-tuple-element.207), channel_id=1, source_target_pairs={{8,0},{16,8},{24,16},{9,1},{17,9},{25,17},{10,2},{18,10},{26,18},{... | collective-permute-start | bytes 196616 | tf_op jit(solution)/shard_map/while/body/eval_jaxpr/ppermute | solution.py:19
  120.4 8.1 %collective-permute-start.10 = (f32[4,32,128]{2,1,0:T(8,128)S(1)}, f32[4,32,128]{2,1,0:T(8,128)S(1)}, u32[]{:S(2)}, u32[]{:S(2)}) collective-permute-start(f32[4,32,128]{2,1,0:T(8,128)S(1)} %get-tuple-element.208), channel_id=1, source_target_pairs={{0,8},{8,16},{16,24},{1,9},{9,17},{17,25},{2,10},{10,18},{18,26},{... | collective-permute-start | bytes 196616 | tf_op jit(solution)/shard_map/while/body/eval_jaxpr/ppermute | solution.py:16
  145.1 33.7 %collective-permute-start.20 = (f32[32,4,128]{2,1,0:T(4,128)S(1)}, f32[32,4,128]{2,1,0:T(4,128)S(1)}, u32[]{:S(2)}, u32[]{:S(2)}) collective-permute-start(f32[32,4,128]{2,1,0:T(4,128)S(1)} %get-tuple-element.171), channel_id=1, source_target_pairs={{1,0},{2,1},{3,2},{4,3},{5,4},{6,5},{7,6},{9,8},{10,9},{11,10},{12... | collective-permute-start | bytes 196616 | tf_op jit(solution)/shard_map/while/body/eval_jaxpr/ppermute | solution.py:19
  146.4 32.4 %collective-permute-start.21 = (f32[32,4,128]{2,1,0:T(4,128)S(1)}, f32[32,4,128]{2,1,0:T(4,128)S(1)}, u32[]{:S(2)}, u32[]{:S(2)}) collective-permute-start(f32[32,4,128]{2,1,0:T(4,128)S(1)} %get-tuple-element.172), channel_id=1, source_target_pairs={{0,1},{1,2},{2,3},{3,4},{4,5},{5,6},{6,7},{8,9},{9,10},{10,11},{11... | collective-permute-start | bytes 196616 | tf_op jit(solution)/shard_map/while/body/eval_jaxpr/ppermute | solution.py:16
  182.2 34.3 %collective-permute-start.23 = (f32[24,4,128]{2,1,0:T(4,128)S(1)}, f32[24,4,128]{2,1,0:T(4,128)}, u32[]{:S(2)}, u32[]{:S(2)}) collective-permute-start(f32[24,4,128]{2,1,0:T(4,128)S(1)} %get-tuple-element.203), channel_id=1, source_target_pairs={{1,0},{2,1},{3,2},{4,3},{5,4},{6,5},{7,6},{9,8},{10,9},{11,10},{12... | collective-permute-start | bytes 147464 | tf_op jit(solution)/shard_map/while/body/eval_jaxpr/ppermute | solution.py:19
  183.5 33.0 %collective-permute-start.22 = (f32[24,4,128]{2,1,0:T(4,128)S(1)}, f32[24,4,128]{2,1,0:T(4,128)}, u32[]{:S(2)}, u32[]{:S(2)}) collective-permute-start(f32[24,4,128]{2,1,0:T(4,128)S(1)} %get-tuple-element.204), channel_id=1, source_target_pairs={{0,1},{1,2},{2,3},{3,4},{4,5},{5,6},{6,7},{8,9},{9,10},{10,11},{11... | collective-permute-start | bytes 147464 | tf_op jit(solution)/shard_map/while/body/eval_jaxpr/ppermute | solution.py:16
  190.7 25.8 %collective-permute-start.19 = (f32[4,32,128]{2,1,0:T(8,128)S(1)}, f32[4,32,128]{2,1,0:T(8,128)S(1)}, u32[]{:S(2)}, u32[]{:S(2)}) collective-permute-start(f32[4,32,128]{2,1,0:T(8,128)S(1)} %get-tuple-element.201), channel_id=1, source_target_pairs={{8,0},{16,8},{24,16},{9,1},{17,9},{25,17},{10,2},{18,10},{26,18},{... | collective-permute-start | bytes 196616 | tf_op jit(solution)/shard_map/while/body/eval_jaxpr/ppermute | solution.py:19
  192.0 24.5 %collective-permute-start.18 = (f32[4,32,128]{2,1,0:T(8,128)S(1)}, f32[4,32,128]{2,1,0:T(8,128)S(1)}, u32[]{:S(2)}, u32[]{:S(2)}) collective-permute-start(f32[4,32,128]{2,1,0:T(8,128)S(1)} %get-tuple-element.202), channel_id=1, source_target_pairs={{0,8},{8,16},{16,24},{1,9},{9,17},{17,25},{2,10},{10,18},{18,26},{... | collective-permute-start | bytes 196616 | tf_op jit(solution)/shard_map/while/body/eval_jaxpr/ppermute | solution.py:16
  271.3 12.0 %collective-permute-start.30 = (f32[24,4,128]{2,1,0:T(4,128)S(1)}, f32[24,4,128]{2,1,0:T(4,128)S(1)}, u32[]{:S(2)}, u32[]{:S(2)}) collective-permute-start(f32[24,4,128]{2,1,0:T(4,128)S(1)} %get-tuple-element.195), channel_id=1, source_target_pairs={{0,1},{1,2},{2,3},{3,4},{4,5},{5,6},{6,7},{8,9},{9,10},{10,11},{11... | collective-permute-start | bytes 147464 | tf_op jit(solution)/shard_map/while/body/eval_jaxpr/ppermute | solution.py:16
  317.5 13.8 %collective-permute-start.38 = (f32[24,4,128]{2,1,0:T(4,128)S(1)}, f32[24,4,128]{2,1,0:T(4,128)S(1)}, u32[]{:S(2)}, u32[]{:S(2)}) collective-permute-start(f32[24,4,128]{2,1,0:T(4,128)S(1)} %get-tuple-element.189), channel_id=1, source_target_pairs={{0,1},{1,2},{2,3},{3,4},{4,5},{5,6},{6,7},{8,9},{9,10},{10,11},{11... | collective-permute-start | bytes 147464 | tf_op jit(solution)/shard_map/while/body/eval_jaxpr/ppermute | solution.py:16
  323.4 8.0 %collective-permute-start.39 = (f32[24,4,128]{2,1,0:T(4,128)S(1)}, f32[24,4,128]{2,1,0:T(4,128)S(1)}, u32[]{:S(2)}, u32[]{:S(2)}) collective-permute-start(f32[24,4,128]{2,1,0:T(4,128)S(1)} %get-tuple-element.190), channel_id=1, source_target_pairs={{1,0},{2,1},{3,2},{4,3},{5,4},{6,5},{7,6},{9,8},{10,9},{11,10},{12... | collective-permute-start | bytes 147464 | tf_op jit(solution)/shard_map/while/body/eval_jaxpr/ppermute | solution.py:19
  362.0 8.0 %collective-permute-start.45 = (f32[32,4,128]{2,1,0:T(4,128)S(1)}, f32[32,4,128]{2,1,0:T(4,128)S(1)}, u32[]{:S(2)}, u32[]{:S(2)}) collective-permute-start(f32[32,4,128]{2,1,0:T(4,128)S(1)} %get-tuple-element.160), channel_id=1, source_target_pairs={{0,1},{1,2},{2,3},{3,4},{4,5},{5,6},{6,7},{8,9},{9,10},{10,11},{11... | collective-permute-start | bytes 196616 | tf_op jit(solution)/shard_map/while/body/eval_jaxpr/ppermute | solution.py:16
  373.0 17.3 %collective-permute-start.42 = (f32[4,32,128]{2,1,0:T(8,128)S(1)}, f32[4,32,128]{2,1,0:T(8,128)S(1)}, u32[]{:S(2)}, u32[]{:S(2)}) collective-permute-start(f32[4,32,128]{2,1,0:T(8,128)S(1)} %get-tuple-element.185), channel_id=1, source_target_pairs={{0,8},{8,16},{16,24},{1,9},{9,17},{17,25},{2,10},{10,18},{18,26},{... | collective-permute-start | bytes 196616 | tf_op jit(solution)/shard_map/while/body/eval_jaxpr/ppermute | solution.py:16
  376.0 14.2 %collective-permute-start.43 = (f32[4,32,128]{2,1,0:T(8,128)S(1)}, f32[4,32,128]{2,1,0:T(8,128)S(1)}, u32[]{:S(2)}, u32[]{:S(2)}) collective-permute-start(f32[4,32,128]{2,1,0:T(8,128)S(1)} %get-tuple-element.186), channel_id=1, source_target_pairs={{8,0},{16,8},{24,16},{9,1},{17,9},{25,17},{10,2},{18,10},{26,18},{... | collective-permute-start | bytes 196616 | tf_op jit(solution)/shard_map/while/body/eval_jaxpr/ppermute | solution.py:19
  (71 other events, 941.8 us)
Sparse Core Ops, SparseCore 0:
  393.7 64.2 reduce-scatter.1
where the time goes:
time: 575 us; the launch traced here: 565 us
  starting transfers between devices  160 us (28%)
  waiting for transfers between devices  103 us (18%)
  local copies, waits for them, and re-layouts  99.9 us (17%)
  blocking collectives  99.8 us (17%)
  other arithmetic  72.8 us (13%)
  between operations  26.6 us (5%)
    ppermute x24, starting transfers between devices, with_halo(): lax.ppermute(lax.slice_in_dim(block, block.shape[dim] - width, None, axis...  129 us
    psum x1, blocking collectives, body(): lax.psum((grad_first, grad_second), ('shot', 'gx', 'gy'))  79 us
    reduce_scatter x1, waiting for transfers between devices, body(): lax.psum_scatter(jnp.stack([totals[0], totals[1]]), 'shot', scatter_dimen...  64.4 us
    gather x3, local copies, waits for them, and re-layouts, one_shot(): pressure[rec_x, rec_y, rec_z] - observed_now[moment]  59.3 us
    unnamed x6, other arithmetic  37.3 us
    ppermute x24, waiting for transfers between devices, with_halo(): lax.ppermute(lax.slice_in_dim(block, 0, width, axis=dim), axis, backward)  32.4 us
    ppermute x24, starting transfers between devices, with_halo(): lax.ppermute(lax.slice_in_dim(block, 0, width, axis=dim), axis, backward)  31.2 us
    all_gather x1, blocking collectives, body(): lax.all_gather(jnp.stack([slab_mod, slab_buoy]), 'shot', axis=3, tiled=True)  20.7 us
  transfers between devices with their start and end apart: 49, of which 14 were waited for; matrix products, arithmetic and copies ran while one was open for 14% of the time, Pallas kernels for 0%

commit v1 on v0

--- a/solution.py
+++ b/solution.py
@@ -222,7 +222,7 @@
     grad_latent, grad_first, grad_second = decoder_grads(
         flattened, hidden, fine_out, shares[0], shares[1], w_first, w_second
     )
-    grad_first, grad_second = lax.psum((grad_first, grad_second), ("shot", "gx", "gy"))
+    grad_first, grad_second = lax.psum(lax.psum((grad_first, grad_second), "shot"), ("gx", "gy"))
     return (grad_latent, grad_first, grad_second)
 
 

time: 575 us -> 665 us (1.16)
  the two profiles are of different devices: /device:TPU:1 before, /device:TPU:0 now
where the time goes in v1:
time: 665 us; the launch traced here: 654 us
  blocking collectives  188 us (28%)
  starting transfers between devices  169 us (25%)
  local copies, waits for them, and re-layouts  100 us (15%)
  waiting for transfers between devices  95.5 us (14%)
  other arithmetic  72.5 us (11%)
  between operations  26.9 us (4%)
    psum x1, blocking collectives, body(): lax.psum(lax.psum((grad_first, grad_second), 'shot'), ('gx', 'gy'))  144 us
    ppermute x24, starting transfers between devices, with_halo(): lax.ppermute(lax.slice_in_dim(block, block.shape[dim] - width, None, axis...  138 us
    gather x3, local copies, waits for them, and re-layouts, one_shot(): pressure[rec_x, rec_y, rec_z] - observed_now[moment]  59.3 us
    reduce_scatter x1, waiting for transfers between devices, body(): lax.psum_scatter(jnp.stack([totals[0], totals[1]]), 'shot', scatter_dimen...  45.3 us
    ppermute x24, waiting for transfers between devices, with_halo(): lax.ppermute(lax.slice_in_dim(block, 0, width, axis=dim), axis, backward)  40.7 us
    unnamed x6, other arithmetic  37.1 us
    ppermute x24, starting transfers between devices, with_halo(): lax.ppermute(lax.slice_in_dim(block, 0, width, axis=dim), axis, backward)  31 us
    psum x1, blocking collectives, body(): lax.psum((grad_first, grad_second), 'shot')  24.5 us
  transfers between devices with their start and end apart: 49, of which 22 were waited for; matrix products, arithmetic and copies ran while one was open for 12% of the time, Pallas kernels for 0%

profile of v1, /device:TPU:0, one launch (start us, length us, event | category | flops | bytes accessed | tf_op | source)
XLA Modules:
  0.0 654.2 jit_solution(12188504431475423485)
XLA Ops:
  33.2 19.9 %all_gather.3 = f32[2,24,32,128]{2,1,0,3:T(8,128)S(1)} all-gather(f32[2,24,32,16]{2,1,0,3:T(8,128)S(1)} %copy.37), channel_id=1, replica_groups=mesh['shot'=8,'gx'=4,'gy'=8] {'shot'}, dimensions={3}, use_global_device_ids=true | all-gather | bytes 884736 | tf_op jit(solution)/shard_map/all_gather | solution.py:165
  67.1 7.1 %collective-permute-start.2 = (f32[4,32,128]{2,1,0:T(8,128)S(1)}, f32[4,32,128]{2,1,0:T(8,128)S(1)}, u32[]{:S(2)}, u32[]{:S(2)}) collective-permute-start(f32[4,32,128]{2,1,0:T(8,128)S(1)} %get-tuple-element.216), channel_id=1, source_target_pairs={{0,8},{8,16},{16,24},{1,9},{9,17},{17,25},{2,10},{10,18},{18,26},{... | collective-permute-start | bytes 196616 | tf_op jit(solution)/shard_map/while/body/eval_jaxpr/ppermute | solution.py:16
  91.5 6.0 collective-permute-start.9
  121.4 6.6 %collective-permute-start.10 = (f32[4,32,128]{2,1,0:T(8,128)S(1)}, f32[4,32,128]{2,1,0:T(8,128)S(1)}, u32[]{:S(2)}, u32[]{:S(2)}) collective-permute-start(f32[4,32,128]{2,1,0:T(8,128)S(1)} %get-tuple-element.210), channel_id=1, source_target_pairs={{0,8},{8,16},{16,24},{1,9},{9,17},{17,25},{2,10},{10,18},{18,26},{... | collective-permute-start | bytes 196616 | tf_op jit(solution)/shard_map/while/body/eval_jaxpr/ppermute | solution.py:16
  134.2 6.0 collective-permute-start.17
  142.2 6.6 %collective-permute-done.16 = f32[4,32,128]{2,1,0:T(8,128)S(1)} collective-permute-done((f32[4,32,128]{2,1,0:T(8,128)S(1)}, f32[4,32,128]{2,1,0:T(8,128)S(1)}, u32[]{:S(2)}, u32[]{:S(2)}) %collective-permute-start.16) | collective-permute-done | bytes 65568 | tf_op jit(solution)/shard_map/while/body/eval_jaxpr/ppermute | solution.py:19
  150.2 6.6 %collective-permute-start.21 = (f32[32,4,128]{2,1,0:T(4,128)S(1)}, f32[32,4,128]{2,1,0:T(4,128)S(1)}, u32[]{:S(2)}, u32[]{:S(2)}) collective-permute-start(f32[32,4,128]{2,1,0:T(4,128)S(1)} %get-tuple-element.174), channel_id=1, source_target_pairs={{0,1},{1,2},{2,3},{3,4},{4,5},{5,6},{6,7},{8,9},{9,10},{10,11},{11... | collective-permute-start | bytes 196616 | tf_op jit(solution)/shard_map/while/body/eval_jaxpr/ppermute | solution.py:16
  157.4 25.6 %gather_fusion.2 = f32[2048]{0:T(1024)} fusion(f32[24,32,128]{2,1,0:T(8,128)S(1)} %scatter-add.39, s32[2048]{0:T(1024)S(1)} %bitcast.153), kind=kCustom, calls=%fused_computation.2 | custom fusion | bytes 40960 | tf_op jit(solution)/shard_map/while/body/eval_jaxpr/gather | solution.py:198
  187.7 7.9 %collective-permute-start.22 = (f32[24,4,128]{2,1,0:T(4,128)S(1)}, f32[24,4,128]{2,1,0:T(4,128)}, u32[]{:S(2)}, u32[]{:S(2)}) collective-permute-start(f32[24,4,128]{2,1,0:T(4,128)S(1)} %get-tuple-element.206), channel_id=1, source_target_pairs={{0,1},{1,2},{2,3},{3,4},{4,5},{5,6},{6,7},{8,9},{9,10},{10,11},{11... | collective-permute-start | bytes 147464 | tf_op jit(solution)/shard_map/while/body/eval_jaxpr/ppermute | solution.py:16
  197.0 6.7 %collective-permute-start.18 = (f32[4,32,128]{2,1,0:T(8,128)S(1)}, f32[4,32,128]{2,1,0:T(8,128)S(1)}, u32[]{:S(2)}, u32[]{:S(2)}) collective-permute-start(f32[4,32,128]{2,1,0:T(8,128)S(1)} %get-tuple-element.204), channel_id=1, source_target_pairs={{0,8},{8,16},{16,24},{1,9},{9,17},{17,25},{2,10},{10,18},{18,26},{... | collective-permute-start | bytes 196616 | tf_op jit(solution)/shard_map/while/body/eval_jaxpr/ppermute | solution.py:16
  205.2 16.9 %gather_fusion.1 = f32[2048]{0:T(1024)S(1)} fusion(f32[24,32,128]{2,1,0:T(8,128)S(1)} %scatter-add.40, s32[2048]{0:T(1024)S(1)} %bitcast.154), kind=kCustom, calls=%fused_computation.1 | custom fusion | bytes 40960 | tf_op jit(solution)/shard_map/while/body/eval_jaxpr/gather | solution.py:198
  227.4 16.9 %gather_fusion = f32[2048]{0:T(1024)S(1)} fusion(f32[24,32,128]{2,1,0:T(8,128)S(1)} %scatter-add.41, s32[2048]{0:T(1024)S(1)} %bitcast.155), kind=kCustom, calls=%fused_computation | custom fusion | bytes 40960 | tf_op jit(solution)/shard_map/while/body/eval_jaxpr/gather | solution.py:198
  245.0 11.9 %scatter_fusion = f32[98304]{0:T(1024)S(1)} fusion(f32[98304]{0:T(1024)S(1)} %bitcast.161, s32[2048]{0:T(1024)S(1)} %broadcast_select_fusion, f32[2048]{0:T(1024)S(1)} %get-tuple-element.229), kind=kCustom, calls=%fused_computation.3 | custom fusion | flops 2048 | bytes 32768
  298.2 11.9 %scatter_fusion.1 = f32[98304]{0:T(1024)S(1)} fusion(f32[98304]{0:T(1024)S(1)} %copy.62, s32[2048]{0:T(1024)S(1)} %broadcast_select_fusion, f32[2048]{0:T(1024)S(1)} %copy-done.34), kind=kCustom, calls=%fused_computation.4 | custom fusion | flops 2048 | bytes 32768
  320.3 6.9 %collective-permute-start.37 = (f32[32,4,128]{2,1,0:T(4,128)S(1)}, f32[32,4,128]{2,1,0:T(4,128)S(1)}, u32[]{:S(2)}, u32[]{:S(2)}) collective-permute-start(f32[32,4,128]{2,1,0:T(4,128)S(1)} %get-tuple-element.166), channel_id=1, source_target_pairs={{0,1},{1,2},{2,3},{3,4},{4,5},{5,6},{6,7},{8,9},{9,10},{10,11},{11... | collective-permute-start | bytes 196616 | tf_op jit(solution)/shard_map/while/body/eval_jaxpr/ppermute | solution.py:16
  329.8 6.4 collective-permute-start.38
  351.3 11.9 %scatter_fusion.2 = f32[98304]{0:T(1024)S(1)} fusion(f32[98304]{0:T(1024)S(1)} %copy.63, s32[2048]{0:T(1024)S(1)} %broadcast_select_fusion, f32[2048]{0:T(1024)S(1)} %copy-done.33), kind=kCustom, calls=%fused_computation.5 | custom fusion | flops 2048 | bytes 32768
  377.7 8.3 %collective-permute-start.45 = (f32[32,4,128]{2,1,0:T(4,128)S(1)}, f32[32,4,128]{2,1,0:T(4,128)S(1)}, u32[]{:S(2)}, u32[]{:S(2)}) collective-permute-start(f32[32,4,128]{2,1,0:T(4,128)S(1)} %get-tuple-element.162), channel_id=1, source_target_pairs={{0,1},{1,2},{2,3},{3,4},{4,5},{5,6},{6,7},{8,9},{9,10},{10,11},{11... | collective-permute-start | bytes 196616 | tf_op jit(solution)/shard_map/while/body/eval_jaxpr/ppermute | solution.py:16
  395.3 6.1 collective-permute-start.46
  403.1 6.8 %collective-permute-done.47 = f32[24,4,128]{2,1,0:T(4,128)S(1)} collective-permute-done((f32[24,4,128]{2,1,0:T(4,128)S(1)}, f32[24,4,128]{2,1,0:T(4,128)S(1)}, u32[]{:S(2)}, u32[]{:S(2)}) %collective-permute-start.47) | collective-permute-done | bytes 49184 | tf_op jit(solution)/shard_map/while/body/eval_jaxpr/ppermute | solution.py:19
  413.3 45.3 %reduce-scatter.2.cloned.1.call-done = f32[2,24,32,16]{2,1,0,3:T(8,128)} async-done(((f32[2,24,32,128]{2,1,0,3:T(8,128)}), f32[2,24,32,16]{2,1,0,3:T(8,128)}) %reduce-scatter.2.cloned.1.call-update) | async-done | bytes 98320 | tf_op jit(solution)/shard_map/reduce_scatter | solution.py:219
  465.3 8.5 %copy.43 = f32[4,6,8,2,4,4,4]{2,1,0,6,5,4,3:T(8,128)} copy(f32[4,6,8,2,4,4,4]{5,2,6,0,4,1,3:T(8,128)S(1)} %maximum_bitcast_fusion) | data formatting | bytes 196608 | tf_op jit(solution)/shard_map/transpose | solution.py:122
  477.5 24.5 %all-reduce.13 = (f32[64,64]{0,1:T(8,128)S(1)}, f32[64,128]{1,0:T(8,128)S(1)}) all-reduce(f32[64,64]{0,1:T(8,128)S(1)} %convolution_bitcast_fusion, f32[64,128]{1,0:T(8,128)S(1)} %fusion.561), channel_id=1, replica_groups=mesh['shot'=8,'gx'=4,'gy'=8] {'shot'}, use_global_device_ids=true, to_apply=%region_5.6 | all-reduce | flops 12288 | bytes 98304 | tf_op jit(solution)/shard_map/psum | solution.py:225
  502.0 143.5 %all-reduce.12 = (f32[64,64]{0,1:T(8,128)S(1)}, f32[64,128]{1,0:T(8,128)}) all-reduce(f32[64,64]{0,1:T(8,128)S(1)} %get-tuple-element.110, f32[64,128]{1,0:T(8,128)S(1)} %get-tuple-element.111), channel_id=1, replica_groups=mesh['shot'=8,'gx'=4,'gy'=8] {'gx','gy'}, use_global_device_ids=true, to_apply=%region_6.7 | all-reduce | flops 12288 | bytes 98304 | tf_op jit(solution)/shard_map/psum | solution.py:225
  (273 shorter events, 202.5 us)
Async XLA Ops:
  7.2 451.4 %reduce-scatter.2.cloned.1.call-start = ((), (), s32[]{:S(2)}) async-start(), calls=%async_computation.1 | async-start | bytes 3538944 | tf_op jit(solution)/shard_map/reduce_scatter | solution.py:219
  8.7 47.6 %collective-permute-start.1 = (f32[4,32,128]{2,1,0:T(8,128)}, f32[4,32,128]{2,1,0:T(8,128)}, u32[]{:S(2)}, u32[]{:S(2)}) collective-permute-start(f32[4,32,128]{2,1,0:T(8,128)} %get-tuple-element.219), channel_id=1, source_target_pairs={{0,8},{8,16},{16,24},{1,9},{9,17},{17,25},{2,10},{10,18},{18,26},{... | collective-permute-start | bytes 196616 | tf_op jit(solution)/shard_map/while/body/eval_jaxpr/ppermute | solution.py:16
  12.8 43.6 %collective-permute-start = (f32[4,32,128]{2,1,0:T(8,128)}, f32[4,32,128]{2,1,0:T(8,128)}, u32[]{:S(2)}, u32[]{:S(2)}) collective-permute-start(f32[4,32,128]{2,1,0:T(8,128)} %get-tuple-element.220), channel_id=1, source_target_pairs={{8,0},{16,8},{24,16},{9,1},{17,9},{25,17},{10,2},{18,10},{26,18},{... | collective-permute-start | bytes 196616 | tf_op jit(solution)/shard_map/while/body/eval_jaxpr/ppermute | solution.py:19
  57.1 17.0 %collective-permute-start.4 = (f32[32,4,128]{2,1,0:T(4,128)S(1)}, f32[32,4,128]{2,1,0:T(4,128)S(1)}, u32[]{:S(2)}, u32[]{:S(2)}) collective-permute-start(f32[32,4,128]{2,1,0:T(4,128)S(1)} %get-tuple-element.181), channel_id=1, source_target_pairs={{1,0},{2,1},{3,2},{4,3},{5,4},{6,5},{7,6},{9,8},{10,9},{11,10},{12... | collective-permute-start | bytes 196616 | tf_op jit(solution)/shard_map/while/body/eval_jaxpr/ppermute | solution.py:19
  58.4 15.7 %collective-permute-start.5 = (f32[32,4,128]{2,1,0:T(4,128)S(1)}, f32[32,4,128]{2,1,0:T(4,128)S(1)}, u32[]{:S(2)}, u32[]{:S(2)}) collective-permute-start(f32[32,4,128]{2,1,0:T(4,128)S(1)} %get-tuple-element.182), channel_id=1, source_target_pairs={{0,1},{1,2},{2,3},{3,4},{4,5},{5,6},{6,7},{8,9},{9,10},{10,11},{11... | collective-permute-start | bytes 196616 | tf_op jit(solution)/shard_map/while/body/eval_jaxpr/ppermute | solution.py:16
  65.8 21.2 %collective-permute-start.3 = (f32[4,32,128]{2,1,0:T(8,128)S(1)}, f32[4,32,128]{2,1,0:T(8,128)S(1)}, u32[]{:S(2)}, u32[]{:S(2)}) collective-permute-start(f32[4,32,128]{2,1,0:T(8,128)S(1)} %get-tuple-element.215), channel_id=1, source_target_pairs={{8,0},{16,8},{24,16},{9,1},{17,9},{25,17},{10,2},{18,10},{26,18},{... | collective-permute-start | bytes 196616 | tf_op jit(solution)/shard_map/while/body/eval_jaxpr/ppermute | solution.py:19
  67.1 19.9 %collective-permute-start.2 = (f32[4,32,128]{2,1,0:T(8,128)S(1)}, f32[4,32,128]{2,1,0:T(8,128)S(1)}, u32[]{:S(2)}, u32[]{:S(2)}) collective-permute-start(f32[4,32,128]{2,1,0:T(8,128)S(1)} %get-tuple-element.216), channel_id=1, source_target_pairs={{0,8},{8,16},{16,24},{1,9},{9,17},{17,25},{2,10},{10,18},{18,26},{... | collective-permute-start | bytes 196616 | tf_op jit(solution)/shard_map/while/body/eval_jaxpr/ppermute | solution.py:16
  77.4 9.6 %collective-permute-start.7 = (f32[24,4,128]{2,1,0:T(4,128)S(1)}, f32[24,4,128]{2,1,0:T(4,128)S(1)}, u32[]{:S(2)}, u32[]{:S(2)}) collective-permute-start(f32[24,4,128]{2,1,0:T(4,128)S(1)} %get-tuple-element.217), channel_id=1, source_target_pairs={{1,0},{2,1},{3,2},{4,3},{5,4},{6,5},{7,6},{9,8},{10,9},{11,10},{12... | collective-permute-start | bytes 147464 | tf_op jit(solution)/shard_map/while/body/eval_jaxpr/ppermute | solution.py:19
  113.9 15.7 %collective-permute-start.15 = (f32[24,4,128]{2,1,0:T(4,128)S(1)}, f32[24,4,128]{2,1,0:T(4,128)S(1)}, u32[]{:S(2)}, u32[]{:S(2)}) collective-permute-start(f32[24,4,128]{2,1,0:T(4,128)S(1)} %get-tuple-element.211), channel_id=1, source_target_pairs={{1,0},{2,1},{3,2},{4,3},{5,4},{6,5},{7,6},{9,8},{10,9},{11,10},{12... | collective-permute-start | bytes 147464 | tf_op jit(solution)/shard_map/while/body/eval_jaxpr/ppermute | solution.py:19
  115.2 14.4 %collective-permute-start.14 = (f32[24,4,128]{2,1,0:T(4,128)S(1)}, f32[24,4,128]{2,1,0:T(4,128)S(1)}, u32[]{:S(2)}, u32[]{:S(2)}) collective-permute-start(f32[24,4,128]{2,1,0:T(4,128)S(1)} %get-tuple-element.212), channel_id=1, source_target_pairs={{0,1},{1,2},{2,3},{3,4},{4,5},{5,6},{6,7},{8,9},{9,10},{10,11},{11... | collective-permute-start | bytes 147464 | tf_op jit(solution)/shard_map/while/body/eval_jaxpr/ppermute | solution.py:16
  120.1 9.5 %collective-permute-start.11 = (f32[4,32,128]{2,1,0:T(8,128)S(1)}, f32[4,32,128]{2,1,0:T(8,128)S(1)}, u32[]{:S(2)}, u32[]{:S(2)}) collective-permute-start(f32[4,32,128]{2,1,0:T(8,128)S(1)} %get-tuple-element.209), channel_id=1, source_target_pairs={{8,0},{16,8},{24,16},{9,1},{17,9},{25,17},{10,2},{18,10},{26,18},{... | collective-permute-start | bytes 196616 | tf_op jit(solution)/shard_map/while/body/eval_jaxpr/ppermute | solution.py:19
  148.9 34.1 %collective-permute-start.20 = (f32[32,4,128]{2,1,0:T(4,128)S(1)}, f32[32,4,128]{2,1,0:T(4,128)S(1)}, u32[]{:S(2)}, u32[]{:S(2)}) collective-permute-start(f32[32,4,128]{2,1,0:T(4,128)S(1)} %get-tuple-element.173), channel_id=1, source_target_pairs={{1,0},{2,1},{3,2},{4,3},{5,4},{6,5},{7,6},{9,8},{10,9},{11,10},{12... | collective-permute-start | bytes 196616 | tf_op jit(solution)/shard_map/while/body/eval_jaxpr/ppermute | solution.py:19
  150.2 32.8 %collective-permute-start.21 = (f32[32,4,128]{2,1,0:T(4,128)S(1)}, f32[32,4,128]{2,1,0:T(4,128)S(1)}, u32[]{:S(2)}, u32[]{:S(2)}) collective-permute-start(f32[32,4,128]{2,1,0:T(4,128)S(1)} %get-tuple-element.174), channel_id=1, source_target_pairs={{0,1},{1,2},{2,3},{3,4},{4,5},{5,6},{6,7},{8,9},{9,10},{10,11},{11... | collective-permute-start | bytes 196616 | tf_op jit(solution)/shard_map/while/body/eval_jaxpr/ppermute | solution.py:16
  186.4 35.6 %collective-permute-start.23 = (f32[24,4,128]{2,1,0:T(4,128)S(1)}, f32[24,4,128]{2,1,0:T(4,128)}, u32[]{:S(2)}, u32[]{:S(2)}) collective-permute-start(f32[24,4,128]{2,1,0:T(4,128)S(1)} %get-tuple-element.205), channel_id=1, source_target_pairs={{1,0},{2,1},{3,2},{4,3},{5,4},{6,5},{7,6},{9,8},{10,9},{11,10},{12... | collective-permute-start | bytes 147464 | tf_op jit(solution)/shard_map/while/body/eval_jaxpr/ppermute | solution.py:19
  187.7 34.3 %collective-permute-start.22 = (f32[24,4,128]{2,1,0:T(4,128)S(1)}, f32[24,4,128]{2,1,0:T(4,128)}, u32[]{:S(2)}, u32[]{:S(2)}) collective-permute-start(f32[24,4,128]{2,1,0:T(4,128)S(1)} %get-tuple-element.206), channel_id=1, source_target_pairs={{0,1},{1,2},{2,3},{3,4},{4,5},{5,6},{6,7},{8,9},{9,10},{10,11},{11... | collective-permute-start | bytes 147464 | tf_op jit(solution)/shard_map/while/body/eval_jaxpr/ppermute | solution.py:16
  195.7 26.4 %collective-permute-start.19 = (f32[4,32,128]{2,1,0:T(8,128)S(1)}, f32[4,32,128]{2,1,0:T(8,128)S(1)}, u32[]{:S(2)}, u32[]{:S(2)}) collective-permute-start(f32[4,32,128]{2,1,0:T(8,128)S(1)} %get-tuple-element.203), channel_id=1, source_target_pairs={{8,0},{16,8},{24,16},{9,1},{17,9},{25,17},{10,2},{18,10},{26,18},{... | collective-permute-start | bytes 196616 | tf_op jit(solution)/shard_map/while/body/eval_jaxpr/ppermute | solution.py:19
  197.0 25.1 %collective-permute-start.18 = (f32[4,32,128]{2,1,0:T(8,128)S(1)}, f32[4,32,128]{2,1,0:T(8,128)S(1)}, u32[]{:S(2)}, u32[]{:S(2)}) collective-permute-start(f32[4,32,128]{2,1,0:T(8,128)S(1)} %get-tuple-element.204), channel_id=1, source_target_pairs={{0,8},{8,16},{16,24},{1,9},{9,17},{17,25},{2,10},{10,18},{18,26},{... | collective-permute-start | bytes 196616 | tf_op jit(solution)/shard_map/while/body/eval_jaxpr/ppermute | solution.py:16
  279.5 12.6 %collective-permute-start.30 = (f32[24,4,128]{2,1,0:T(4,128)S(1)}, f32[24,4,128]{2,1,0:T(4,128)S(1)}, u32[]{:S(2)}, u32[]{:S(2)}) collective-permute-start(f32[24,4,128]{2,1,0:T(4,128)S(1)} %get-tuple-element.197), channel_id=1, source_target_pairs={{0,1},{1,2},{2,3},{3,4},{4,5},{5,6},{6,7},{8,9},{9,10},{10,11},{11... | collective-permute-start | bytes 147464 | tf_op jit(solution)/shard_map/while/body/eval_jaxpr/ppermute | solution.py:16
  320.3 8.8 %collective-permute-start.37 = (f32[32,4,128]{2,1,0:T(4,128)S(1)}, f32[32,4,128]{2,1,0:T(4,128)S(1)}, u32[]{:S(2)}, u32[]{:S(2)}) collective-permute-start(f32[32,4,128]{2,1,0:T(4,128)S(1)} %get-tuple-element.166), channel_id=1, source_target_pairs={{0,1},{1,2},{2,3},{3,4},{4,5},{5,6},{6,7},{8,9},{9,10},{10,11},{11... | collective-permute-start | bytes 196616 | tf_op jit(solution)/shard_map/while/body/eval_jaxpr/ppermute | solution.py:16
  329.8 15.0 %collective-permute-start.38 = (f32[24,4,128]{2,1,0:T(4,128)S(1)}, f32[24,4,128]{2,1,0:T(4,128)S(1)}, u32[]{:S(2)}, u32[]{:S(2)}) collective-permute-start(f32[24,4,128]{2,1,0:T(4,128)S(1)} %get-tuple-element.191), channel_id=1, source_target_pairs={{0,1},{1,2},{2,3},{3,4},{4,5},{5,6},{6,7},{8,9},{9,10},{10,11},{11... | collective-permute-start | bytes 147464 | tf_op jit(solution)/shard_map/while/body/eval_jaxpr/ppermute | solution.py:16
  376.4 9.9 %collective-permute-start.44 = (f32[32,4,128]{2,1,0:T(4,128)S(1)}, f32[32,4,128]{2,1,0:T(4,128)S(1)}, u32[]{:S(2)}, u32[]{:S(2)}) collective-permute-start(f32[32,4,128]{2,1,0:T(4,128)S(1)} %get-tuple-element.161), channel_id=1, source_target_pairs={{1,0},{2,1},{3,2},{4,3},{5,4},{6,5},{7,6},{9,8},{10,9},{11,10},{12... | collective-permute-start | bytes 196616 | tf_op jit(solution)/shard_map/while/body/eval_jaxpr/ppermute | solution.py:19
  377.7 10.2 %collective-permute-start.45 = (f32[32,4,128]{2,1,0:T(4,128)S(1)}, f32[32,4,128]{2,1,0:T(4,128)S(1)}, u32[]{:S(2)}, u32[]{:S(2)}) collective-permute-start(f32[32,4,128]{2,1,0:T(4,128)S(1)} %get-tuple-element.162), channel_id=1, source_target_pairs={{0,1},{1,2},{2,3},{3,4},{4,5},{5,6},{6,7},{8,9},{9,10},{10,11},{11... | collective-permute-start | bytes 196616 | tf_op jit(solution)/shard_map/while/body/eval_jaxpr/ppermute | solution.py:16
  390.8 19.1 %collective-permute-start.42 = (f32[4,32,128]{2,1,0:T(8,128)S(1)}, f32[4,32,128]{2,1,0:T(8,128)S(1)}, u32[]{:S(2)}, u32[]{:S(2)}) collective-permute-start(f32[4,32,128]{2,1,0:T(8,128)S(1)} %get-tuple-element.187), channel_id=1, source_target_pairs={{0,8},{8,16},{16,24},{1,9},{9,17},{17,25},{2,10},{10,18},{18,26},{... | collective-permute-start | bytes 196616 | tf_op jit(solution)/shard_map/while/body/eval_jaxpr/ppermute | solution.py:16
  394.0 15.9 %collective-permute-start.43 = (f32[4,32,128]{2,1,0:T(8,128)S(1)}, f32[4,32,128]{2,1,0:T(8,128)S(1)}, u32[]{:S(2)}, u32[]{:S(2)}) collective-permute-start(f32[4,32,128]{2,1,0:T(8,128)S(1)} %get-tuple-element.188), channel_id=1, source_target_pairs={{8,0},{16,8},{24,16},{9,1},{17,9},{25,17},{10,2},{18,10},{26,18},{... | collective-permute-start | bytes 196616 | tf_op jit(solution)/shard_map/while/body/eval_jaxpr/ppermute | solution.py:19
  (71 other events, 1001.1 us)
Sparse Core Ops, SparseCore 0:
  413.4 45.1 reduce-scatter.1
